TPU v7x, 256 devices: a whole 4x4x8 slice. The times are simulated.
256 devices in a mesh: row: 8 (over y_lo, x), col: 4 (over y_hi, core), dep: 8 (over z).
Axes of the slice: x: 4, y: 4 (y_hi: 2, y_lo: 2; y = y_hi * 2 + y_lo), z: 8, core: 2. Of those that a mesh axis runs over, the one named last changes fastest.
Arguments:
- tokens_in: bfloat16 [8, 384, 6144], P('dep', None, 'row'), may hold values from -6 to 6
- weight: bfloat16 [6144, 24576], P('row', 'col'), may hold values from -0.078125 to 0.078125
- cotangent: bfloat16 [8, 384, 24576], P('dep', 'row', 'col'), may hold values from -6 to 6
Outputs:
- activated: bfloat16 [8, 384, 24576], P('dep', 'row', 'col')
- input_grad: bfloat16 [8, 384, 6144], P('dep', 'col', 'row')
- weight_grad: bfloat16 [6144, 24576], P(('row', 'dep'), 'col')
All inputs are finite; a program needn't handle non-finite values.
Results may differ from a plain program's by a relative error of at most 0.023.
Values may be sent and summed in bfloat16 or wider, within the bound.
A program may use at most 128 MiB of HBM per device.

v0:
```python
import math

import jax
import jax.numpy as jnp
from jax import lax
from jax.sharding import PartitionSpec as P

root_coef = math.sqrt(2.0 / math.pi)


def slope_of(value):
    inner = root_coef * (value + 0.044715 * value * value * value)
    tangent = jnp.tanh(inner)
    return 0.5 * (1.0 + tangent) + 0.5 * value * (1.0 - tangent * tangent) * root_coef * (
        1.0 + 3.0 * 0.044715 * value * value
    )


def body(tokens_in, weight, cotangent):
    local_tokens = tokens_in[0]
    group_rows = local_tokens.shape[0]
    scale = 1.0 / math.sqrt(group_rows * lax.axis_size("dep"))
    rows = local_tokens
    pre_act = lax.psum_scatter(
        jnp.dot(rows, weight, preferred_element_type=jnp.float32).astype(jnp.bfloat16),
        "row",
        scatter_dimension=0,
        tiled=True,
    ).astype(jnp.float32)
    activated = jax.nn.gelu(pre_act, approximate=True).astype(jnp.bfloat16)
    hidden_grad = (cotangent[0].astype(jnp.float32) * slope_of(pre_act)).astype(jnp.bfloat16)
    grad_rows = lax.all_gather(hidden_grad, "row", axis=0, tiled=True)
    rows = grad_rows
    summed = lax.psum_scatter(
        lax.dot_general(
            rows, weight, (((1,), (1,)), ((), ())), preferred_element_type=jnp.float32
        ).astype(jnp.bfloat16),
        "col",
        scatter_dimension=0,
        tiled=True,
    ).astype(jnp.float32)
    input_grad = summed.astype(jnp.bfloat16)
    product = lax.dot_general(
        local_tokens, grad_rows, (((0,), (0,)), ((), ())), preferred_element_type=jnp.float32
    )
    summed = lax.psum_scatter(
        (product * scale).astype(jnp.bfloat16), "dep", scatter_dimension=0, tiled=True
    ).astype(jnp.float32)
    weight_grad = summed.astype(jnp.bfloat16)
    return (activated[None], input_grad[None], weight_grad)


def solution(mesh):
    in_specs = (P("dep", None, "row"), P("row", "col"), P("dep", "row", "col"))
    out_specs = (P("dep", "row", "col"), P("dep", "col", "row"), P(("row", "dep"), "col"))
    return jax.shard_map(body, mesh=mesh, in_specs=in_specs, out_specs=out_specs, check_vma=False)
```

profile of v0, /device:TPU:32, one launch (start us, length us, event | category | flops | bytes accessed | tf_op | source)
XLA Modules:
  0.0 298.0 jit_solution(8590639339700753710)
XLA Ops:
  7.2 0.0 copy-start
  7.2 0.0 reduce-scatter.6.cloned.1.call-start
  7.2 1.0 copy-done
  8.2 9.1 %convolution_convert_fusion = bf16[384,6144]{1,0:T(8,128)(2,1)} fusion(bf16[768,6144]{1,0:T(8,128)(2,1)} %param.4, bf16[1,384,768]{2,1,0:T(8,128)(2,1)S(1)} %copy-done), kind=kOutput, calls=%fused_computation.2 | convolution fusion | flops 3626237952 | bytes 14745600 | tf_op jit(solution)/shard_map/dot_general | solution.py:25
  17.4 0.0 copy-start.1
  17.4 0.0 reduce-scatter.6.cloned.1.call-update
  17.4 0.0 all-gather.2.cloned.1.call-start
  17.4 63.3 %reduce-scatter.6.cloned.1.call-done = bf16[48,6144]{1,0:T(8,128)(2,1)} async-done(((bf16[384,6144]{1,0:T(8,128)(2,1)}), bf16[48,6144]{1,0:T(8,128)(2,1)}) %reduce-scatter.6.cloned.1.call-update) | async-done | bytes 589840 | tf_op jit(solution)/shard_map/reduce_scatter | solution.py:24
  80.7 0.0 copy-done.1
  80.7 3.3 %fusion.14 = (bf16[48,6144]{1,0:T(8,128)(2,1)}, bf16[1,48,6144]{2,1,0:T(8,128)(2,1)}) fusion(bf16[48,6144]{1,0:T(8,128)(2,1)} %reduce-scatter.6.cloned.1.call-done, bf16[1,48,6144]{2,1,0:T(8,128)(2,1)S(1)} %copy-done.1), kind=kLoop, calls=%fused_computation.28 | loop fusion | flops 8847360 | bytes 2359296 | tf_op jit(solution)/shard_map/convert_element_type | solution.py:31
  83.9 0.0 all-gather.2.cloned.1.call-update
  84.0 0.0 reduce-scatter.8.cloned.1.call-start
  84.0 59.0 %all-gather.2.cloned.1.call-done = bf16[384,6144]{1,0:T(8,128)(2,1)} async-done(((bf16[48,6144]{1,0:T(8,128)(2,1)}), bf16[384,6144]{1,0:T(8,128)(2,1)}) %all-gather.2.cloned.1.call-update) | async-done | bytes 4718608 | tf_op jit(solution)/shard_map/all_gather | solution.py:32
  143.0 9.8 %convolution_convert_fusion.1 = bf16[384,768]{1,0:T(8,128)(2,1)} fusion(bf16[384,6144]{1,0:T(8,128)(2,1)} %all-gather.2.cloned.1.call-done, bf16[768,6144]{1,0:T(8,128)(2,1)} %param.4), kind=kOutput, calls=%fused_computation.14 | convolution fusion | flops 3624173568 | bytes 14745600 | tf_op jit(solution)/shard_map/dot_general | solution.py:35
  152.8 0.0 reduce-scatter.8.cloned.1.call-update
  152.8 0.0 reduce-scatter.10.cloned.1.call-start
  152.9 9.7 %fusion = bf16[768,6144]{0,1:T(8,128)(2,1)} fusion(bf16[384,6144]{1,0:T(8,128)(2,1)} %all-gather.2.cloned.1.call-done, bf16[1,384,768]{2,1,0:T(8,128)(2,1)S(1)} %copy-done), kind=kOutput, calls=%fused_computation.1 | convolution fusion | flops 3633315840 | bytes 14745600 | tf_op jit(solution)/shard_map/dot_general | solution.py:43
  162.6 12.7 %copy.8 = bf16[768,6144]{1,0:T(8,128)(2,1)} copy(bf16[768,6144]{0,1:T(8,128)(2,1)} %fusion) | data formatting | bytes 18874368
  175.3 0.0 reduce-scatter.10.cloned.1.call-update
  175.3 10.7 %reduce-scatter.8.cloned.1.call-done = bf16[96,768]{1,0:T(8,128)(2,1)} async-done(((bf16[384,768]{1,0:T(8,128)(2,1)}), bf16[96,768]{1,0:T(8,128)(2,1)}) %reduce-scatter.8.cloned.1.call-update) | async-done | bytes 147472 | tf_op jit(solution)/shard_map/reduce_scatter | solution.py:34
  186.0 105.5 %reduce-scatter.10.cloned.1.call-done = bf16[96,6144]{1,0:T(8,128)(2,1)} async-done(((bf16[768,6144]{1,0:T(8,128)(2,1)}), bf16[96,6144]{1,0:T(8,128)(2,1)}) %reduce-scatter.10.cloned.1.call-update) | async-done | bytes 1179664
Async XLA Ops:
  7.2 1.1 copy-start
  7.2 73.5 %reduce-scatter.6.cloned.1.call-start = ((), (), s32[]{:S(2)}) async-start(), calls=%async_computation.3 | async-start | bytes 5308416 | tf_op jit(solution)/shard_map/reduce_scatter | solution.py:24
  17.4 63.3 %copy-start.1 = (bf16[1,48,6144]{2,1,0:T(8,128)(2,1)S(1)}, bf16[1,48,6144]{2,1,0:T(8,128)(2,1)}, u32[]{:S(2)}) copy-start(bf16[1,48,6144]{2,1,0:T(8,128)(2,1)} %param.5) | copy-start | bytes 1769476
  17.4 125.6 %all-gather.2.cloned.1.call-start = ((), (), s32[]{:S(2)}) async-start(), calls=%async_computation.4 | async-start | bytes 5308416 | tf_op jit(solution)/shard_map/all_gather | solution.py:32
  84.0 102.0 %reduce-scatter.8.cloned.1.call-start = ((), (), s32[]{:S(2)}) async-start(), calls=%async_computation.5 | async-start | bytes 737280 | tf_op jit(solution)/shard_map/reduce_scatter | solution.py:34
  152.8 138.6 %reduce-scatter.10.cloned.1.call-start = ((), (), s32[]{:S(2)}) async-start(), calls=%async_computation.6 | async-start | bytes 10616832
Sparse Core Ops, SparseCore 0:
  17.5 63.1 reduce-scatter.5
  84.1 58.8 all-gather.1
  153.0 32.9 reduce-scatter.7
  188.9 102.4 reduce-scatter.9
where the time goes:
time: 302 us; the launch traced here: 298 us
  waiting for transfers between devices  238 us (79%)
  matrix products  28.6 us (9%)
  between operations  13.8 us (5%)
  local copies, waits for them, and re-layouts  13.7 us (5%)
  other arithmetic  3.25 us (1%)
    unnamed x5, waiting for transfers between devices  106 us
    reduce_scatter x1, waiting for transfers between devices, body(): lax.psum_scatter(jnp.dot(rows, weight, preferred_element_type=jnp.float32...  63.3 us
    all_gather x1, waiting for transfers between devices, body(): grad_rows = lax.all_gather(hidden_grad, 'row', axis=0, tiled=True)  59 us
    unnamed x5, local copies, waits for them, and re-layouts  13.7 us
    reduce_scatter x1, waiting for transfers between devices, body(): lax.psum_scatter(lax.dot_general(rows, weight, (((1,), (1,)), ((), ())),...  10.7 us
    dot_general x1, matrix products, body(): lax.dot_general(rows, weight, (((1,), (1,)), ((), ())), preferred_element...  9.79 us
    dot_general x1, matrix products, body(): lax.dot_general(local_tokens, grad_rows, (((0,), (0,)), ((), ())), prefer...  9.68 us
    dot_general x1, matrix products, body(): jnp.dot(rows, weight, preferred_element_type=jnp.float32)  9.13 us
  transfers between devices with their start and end apart: 4, of which 4 were waited for; matrix products, arithmetic and copies ran while one was open for 8% of the time, Pallas kernels for 0%

commit v1 on v0

v1 whole, which is shorter than its diff:
```python
import functools
import math

import jax
import jax.numpy as jnp
from jax import lax
from jax.experimental import pallas as pl
from jax.experimental.pallas import tpu as pltpu
from jax.sharding import PartitionSpec as P

MESH = pl.DeviceIdType.MESH
F32 = jnp.float32
BF16 = jnp.bfloat16

CHUNKS = 8

root_coef = math.sqrt(2.0 / math.pi)

RS1, RS2, RSY, AGY, AGX1, AGX2, Z1, Z2, Z3, Z4 = 0, 2, 4, 5, 6, 8, 10, 12, 14, 16
COPIES = 18


def kernel(
    scale, chunks,
    tok_hbm, w_hbm, cot_hbm, act_hbm, ig_hbm, wg_hbm,
    tok, tok_t, w, cot, part, r1, r2, y_out, y_in, own, hid, grad, z1_in, z_in,
    acc, ig_out, ig_in, ig_own, act, wg,
    send, recv, col_send, col_recv, load_w, load_cot, load_tok, store_act, store_wg, store_ig,
):
    width = w.shape[2]
    half = width // 2
    left_half, right_half = pl.ds(0, half), pl.ds(half, half)
    row, col, dep = lax.axis_index("row"), lax.axis_index("col"), lax.axis_index("dep")
    x, y = lax.rem(row, 4), row // 4
    other_y = 1 - y
    xr, xo, xl = lax.rem(x + 1, 4), lax.rem(x + 2, 4), lax.rem(x + 3, 4)
    right, left = {"row": y * 4 + xr}, {"row": y * 4 + xl}
    across = {"row": other_y * 4 + x}
    at = [lax.rem(dep + k, 8) for k in range(8)]
    up, down = {"dep": at[1]}, {"dep": at[7]}
    col_peers = [{"col": lax.rem(col + j, 4)} for j in (1, 2, 3)]

    def columns(c):
        return pl.ds(pl.multiple_of(c * width, 128), width)

    def tok_copy():
        return pltpu.make_async_copy(tok_hbm.at[0], tok, load_tok)

    def w_copy(c):
        return pltpu.make_async_copy(w_hbm.at[:, columns(c)], w.at[c], load_w.at[c])

    def cot_copy(c):
        return pltpu.make_async_copy(cot_hbm.at[0, :, columns(c)], cot.at[c], load_cot.at[c])

    tok_copy().start()

    @pl.loop(0, chunks)
    def _(c):
        w_copy(c).start()

    @pl.loop(0, chunks)
    def _(c):
        cot_copy(c).start()

    barrier = pltpu.get_barrier_semaphore()
    peers = [right, left, across, up, down] + col_peers
    for peer in peers:
        pl.semaphore_signal(barrier, inc=1, device_id=peer, device_id_type=MESH)

    def act_copy(c):
        return pltpu.make_async_copy(act.at[c], act_hbm.at[0, :, columns(c)], store_act.at[c])

    def wg_copy(c):
        return pltpu.make_async_copy(wg.at[c], wg_hbm.at[:, columns(c)], store_wg.at[c])

    def ig_copy():
        return pltpu.make_async_copy(ig_own, ig_hbm.at[0], store_ig)

    def remote(c, which, source, target, device):
        return pltpu.make_async_remote_copy(
            src_ref=source, dst_ref=target, send_sem=send.at[c, which], recv_sem=recv.at[c, which],
            device_id=device, device_id_type=MESH,
        )

    def rs1(c):
        return (
            remote(c, RS1, part.at[c, :, xo, :, left_half], r1.at[c, 0], right),
            remote(c, RS1 + 1, part.at[c, :, xo, :, right_half], r1.at[c, 1], left),
        )

    def rs2(c):
        return (
            remote(c, RS2, part.at[c, :, xr], r2.at[c, 0], right),
            remote(c, RS2 + 1, part.at[c, :, xl], r2.at[c, 1], left),
        )

    def rsy(c):
        return (remote(c, RSY, y_out.at[c], y_in.at[c], across),)

    def agy(c):
        return (remote(c, AGY, hid.at[c, y, x], hid.at[c, y, x], across),)

    def agx1(c):
        return (
            remote(c, AGX1, hid.at[c, :, x], hid.at[c, :, x], right),
            remote(c, AGX1 + 1, hid.at[c, :, x], hid.at[c, :, x], left),
        )

    def agx2(c):
        return (
            remote(c, AGX2, hid.at[c, :, xl, :, left_half], hid.at[c, :, xl, :, left_half], right),
            remote(c, AGX2 + 1, hid.at[c, :, xr, :, right_half], hid.at[c, :, xr, :, right_half], left),
        )

    def z1(c):
        return (
            remote(c, Z1, grad.at[c, at[4], :, left_half], z1_in.at[c, 0], up),
            remote(c, Z1 + 1, grad.at[c, at[4], :, right_half], z1_in.at[c, 1], down),
        )

    def z_step(c, which, step, above, below):
        return (
            remote(c, which, grad.at[c, above], z_in.at[c, step, 0], up),
            remote(c, which + 1, grad.at[c, below], z_in.at[c, step, 1], down),
        )

    def z2(c):
        return z_step(c, Z2, 0, at[3], at[5])

    def z3(c):
        return z_step(c, Z3, 1, at[2], at[6])

    def z4(c):
        return z_step(c, Z4, 2, at[1], at[7])

    def start(copies):
        for copy in copies:
            copy.start()

    def arrived(copies):
        for copy in copies:
            copy.wait_recv()

    def col_copy(j):
        return pltpu.make_async_remote_copy(
            src_ref=ig_out.at[lax.rem(col + j, 4)], dst_ref=ig_in.at[j - 1],
            send_sem=col_send.at[j - 1], recv_sem=col_recv.at[j - 1],
            device_id=col_peers[j - 1], device_id_type=MESH,
        )

    def f32(value):
        return value.astype(F32)

    def project(c):
        w_copy(c).wait()
        block = jnp.dot(tok[...], w[c], preferred_element_type=F32).astype(BF16)
        part[c] = block.reshape(part.shape[1:])
        start(rs1(c))

    def row_second(c):
        arrived(rs1(c))
        part[c, :, xr, :, left_half] = (f32(part[c, :, xr, :, left_half]) + f32(r1[c, 0])).astype(BF16)
        part[c, :, xl, :, right_half] = (f32(part[c, :, xl, :, right_half]) + f32(r1[c, 1])).astype(BF16)
        start(rs2(c))

    def row_across(c):
        arrived(rs2(c))
        y_out[c] = (f32(part[c, other_y, x]) + f32(r2[c, 0, other_y]) + f32(r2[c, 1, other_y])).astype(BF16)
        start(rsy(c))
        own[c] = f32(part[c, y, x]) + f32(r2[c, 0, y]) + f32(r2[c, 1, y])

    def activate(c):
        arrived(rsy(c))
        cot_copy(c).wait()
        value = own[c] + f32(y_in[c])
        square = value * value
        tangent = jnp.tanh(root_coef * (value + 0.044715 * value * square))
        slope = 0.5 * (1.0 + tangent) + 0.5 * value * (1.0 - tangent * tangent) * root_coef * (
            1.0 + 3.0 * 0.044715 * square
        )
        hid[c, y, x] = (f32(cot[c]) * slope).astype(BF16)
        start(agy(c))
        act[c] = (0.5 * value * (1.0 + tangent)).astype(BF16)
        act_copy(c).start()

    def gather_first(c):
        arrived((remote(c, AGY, hid.at[c, other_y, x], hid.at[c, other_y, x], across),))
        start(agx1(c))

    def gather_second(c):
        arrived((
            remote(c, AGX1, hid.at[c, :, xl], hid.at[c, :, xl], right),
            remote(c, AGX1 + 1, hid.at[c, :, xr], hid.at[c, :, xr], left),
        ))
        start(agx2(c))

    def weight_first(c):
        arrived((
            remote(c, AGX2, hid.at[c, :, xo, :, left_half], hid.at[c, :, xo, :, left_half], right),
            remote(c, AGX2 + 1, hid.at[c, :, xo, :, right_half], hid.at[c, :, xo, :, right_half], left),
        ))
        rows = hid[c].reshape(-1, width)
        product = jnp.dot(tok_t[...], rows, preferred_element_type=F32)
        grad[c] = (product * scale).astype(BF16).reshape(grad.shape[1:])
        start(z1(c))

    def input_part(c):
        rows = hid[c].reshape(-1, width)
        acc[...] += lax.dot_general(rows, w[c], (((1,), (1,)), ((), ())), preferred_element_type=F32)

        @pl.when(c == chunks - 1)
        def _():
            ig_out[...] = acc[...].astype(BF16).reshape(ig_out.shape)
            for j in (1, 2, 3):
                col_copy(j).start()

    def weight_second(c):
        arrived(z1(c))
        grad[c, at[3], :, left_half] = (f32(grad[c, at[3], :, left_half]) + f32(z1_in[c, 0])).astype(BF16)
        grad[c, at[5], :, right_half] = (f32(grad[c, at[5], :, right_half]) + f32(z1_in[c, 1])).astype(BF16)
        start(z2(c))

    def weight_third(c):
        arrived(z2(c))
        grad[c, at[2]] = (f32(grad[c, at[2]]) + f32(z_in[c, 0, 0])).astype(BF16)
        grad[c, at[6]] = (f32(grad[c, at[6]]) + f32(z_in[c, 0, 1])).astype(BF16)
        start(z3(c))

    def weight_fourth(c):
        arrived(z3(c))
        grad[c, at[1]] = (f32(grad[c, at[1]]) + f32(z_in[c, 1, 0])).astype(BF16)
        grad[c, at[7]] = (f32(grad[c, at[7]]) + f32(z_in[c, 1, 1])).astype(BF16)
        start(z4(c))

    def weight_last(c):
        arrived(z4(c))
        wg[c] = (f32(grad[c, dep]) + f32(z_in[c, 2, 0]) + f32(z_in[c, 2, 1])).astype(BF16)
        wg_copy(c).start()

    tok_copy().wait()
    tok_t[...] = tok[...].T
    acc[...] = jnp.zeros_like(acc)
    pl.semaphore_wait(barrier, len(peers))

    order = (
        (weight_first, 2), (activate, 1), (project, 0), (input_part, 2),
        (weight_third, 3), (gather_first, 1),
        (weight_second, 2), (row_second, 0),
        (weight_fourth, 3), (gather_second, 1), (row_across, 0), (weight_last, 4),
    )
    slots = max(late for _, late in order)

    @pl.loop(0, chunks + slots)
    def _(t):
        for stage, late in order:
            c = t - late

            @pl.when((c >= 0) & (c < chunks))
            def _(stage=stage, c=c):
                stage(c)

    for j in (1, 2, 3):
        col_copy(j).wait_recv()
    tokens = ig_own.shape[0]
    mine = acc[pl.ds(pl.multiple_of(col * tokens, 8), tokens), :]
    ig_own[...] = (mine + f32(ig_in[0]) + f32(ig_in[1]) + f32(ig_in[2])).astype(BF16)
    ig_copy().start()

    @pl.loop(0, chunks)
    def _(c):
        for copies in (rs1, rs2, rsy, agy, agx1, agx2, z1, z2, z3, z4):
            for copy in copies(c):
                copy.wait_send()
        act_copy(c).wait()
        wg_copy(c).wait()

    for j in (1, 2, 3):
        col_copy(j).wait_send()
    ig_copy().wait()


def body(chunks, tokens_in, weight, cotangent):
    tokens, features = tokens_in.shape[1:]
    hidden = weight.shape[1]
    own_tokens = cotangent.shape[1]
    scale = 1.0 / math.sqrt(tokens * lax.axis_size("dep"))
    c, w = chunks, hidden // chunks
    h = w // 2
    own_features, col_tokens = features // 8, tokens // 4
    vmem = pltpu.VMEM
    dma = pltpu.SemaphoreType.DMA
    return pl.pallas_call(
        functools.partial(kernel, scale, chunks),
        out_shape=(
            jax.ShapeDtypeStruct((1, own_tokens, hidden), BF16),
            jax.ShapeDtypeStruct((1, col_tokens, features), BF16),
            jax.ShapeDtypeStruct((own_features, hidden), BF16),
        ),
        in_specs=[pl.BlockSpec(memory_space=pl.ANY)] * 3,
        out_specs=(pl.BlockSpec(memory_space=pl.ANY),) * 3,
        scratch_shapes=[
            vmem((tokens, features), BF16),
            vmem((features, tokens), BF16),
            vmem((c, features, w), BF16),
            vmem((c, own_tokens, w), BF16),
            vmem((c, 2, 4, own_tokens, w), BF16),
            vmem((c, 2, 2, own_tokens, h), BF16),
            vmem((c, 2, 2, own_tokens, w), BF16),
            vmem((c, own_tokens, w), BF16),
            vmem((c, own_tokens, w), BF16),
            vmem((c, own_tokens, w), F32),
            vmem((c, 2, 4, own_tokens, w), BF16),
            vmem((c, 8, own_features, w), BF16),
            vmem((c, 2, own_features, h), BF16),
            vmem((c, 3, 2, own_features, w), BF16),
            vmem((tokens, features), F32),
            vmem((4, col_tokens, features), BF16),
            vmem((3, col_tokens, features), BF16),
            vmem((col_tokens, features), BF16),
            vmem((c, own_tokens, w), BF16),
            vmem((c, own_features, w), BF16),
            dma((c, COPIES)),
            dma((c, COPIES)),
            dma((3,)),
            dma((3,)),
            dma((c,)),
            dma((c,)),
            dma,
            dma((c,)),
            dma((c,)),
            dma,
        ],
        compiler_params=pltpu.CompilerParams(
            collective_id=0, has_side_effects=True, vmem_limit_bytes=60 * 1024 * 1024
        ),
        cost_estimate=pl.CostEstimate(
            flops=6 * tokens * features * hidden,
            bytes_accessed=2 * (features * hidden + 2 * own_tokens * hidden + tokens * features),
            transcendentals=own_tokens * hidden,
        ),
    )(tokens_in, weight, cotangent)


def solution(mesh):
    in_specs = (P("dep", None, "row"), P("row", "col"), P("dep", "row", "col"))
    out_specs = (P("dep", "row", "col"), P("dep", "col", "row"), P(("row", "dep"), "col"))
    return jax.shard_map(
        functools.partial(body, CHUNKS), mesh=mesh, in_specs=in_specs, out_specs=out_specs, check_vma=False
    )
```

time: 302 us -> 167 us (0.55); the launches traced: 298 us -> 167 us
  waiting for transfers between devices: 238 us -> 0 us
  Pallas kernels: 0 us -> 162 us
  matrix products: 28.6 us -> 0 us
  between operations: 13.8 us -> 0.65 us
  local copies, waits for them, and re-layouts: 13.7 us -> 4.61 us
  other arithmetic: 3.25 us -> 0 us
    pallas_call x0 -> x1, Pallas kernels: none -> 162 us  [body(): pl.pallas_call(functools.partial(kernel, scale, chunks), out_shape=(jax.S...]
    unnamed x5 -> x0, waiting for transfers between devices: 106 us -> none
    reduce_scatter x2 -> x0, waiting for transfers between devices: 73.9 us -> none  [the longest x1 63.3 us: body(): lax.psum_scatter(jnp.dot(rows, weight, preferred_element_type=jnp.float32...]
    all_gather x1 -> x0, waiting for transfers between devices: 59 us -> none  [body(): grad_rows = lax.all_gather(hidden_grad, 'row', axis=0, tiled=True)]
    dot_general x3 -> x0, matrix products: 28.6 us -> none  [the longest x1 9.79 us: body(): lax.dot_general(rows, weight, (((1,), (1,)), ((), ())), preferred_element...]
    unnamed x5, local copies, waits for them, and re-layouts: 13.7 us -> 4.61 us
    convert_element_type x1 -> x0, other arithmetic: 3.25 us -> none  [body(): (cotangent[0].astype(jnp.float32) * slope_of(pre_act)).astype(jnp.bfloat16)]
  transfers between devices with their start and end apart: 4 -> 0, of which waited for: 4 -> 0; matrix products, arithmetic and copies ran while one was open for 8% -> 0% of each run, Pallas kernels for 0% -> 0%
where the time goes in v1:
time: 167 us
  Pallas kernels  162 us (97%)
  local copies, waits for them, and re-layouts  4.61 us (3%)
    pallas_call x1, Pallas kernels, body(): pl.pallas_call(functools.partial(kernel, scale, chunks), out_shape=(jax.S...  162 us
    unnamed x5, local copies, waits for them, and re-layouts  4.61 us

profile of v1, /device:TPU:32, one launch (start us, length us, event | category | flops | bytes accessed | tf_op | source)
XLA Modules:
  0.0 167.0 jit_solution(3472869991994588762)
XLA Ops:
  0.6 161.8 %shard_map.58 = (bf16[1,48,6144]{2,1,0:T(8,128)(2,1)}, bf16[1,96,768]{2,1,0:T(8,128)(2,1)}, bf16[96,6144]{1,0:T(8,128)(2,1)}) custom-call(bf16[1,384,768]{2,1,0:T(8,128)(2,1)} %tok_hbm.1, bf16[768,6144]{1,0:T(8,128)(2,1)} %w_hbm.1, bf16[1,48,6144]{2,1,0:T(8,128)(2,1)} %cot_hbm.1), custom_call_target="tpu_custom_call" | custom-call | flops 10871635968 | bytes 11206656 | tf_op jit(solution)/shard_map/pallas_call | solution.py:292
  162.4 0.0 copy-start
  162.4 2.0 %copy.9 = bf16[1,48,6144]{2,1,0:T(8,128)(2,1)} copy(bf16[1,48,6144]{2,1,0:T(8,128)(2,1)} %get-tuple-element.6) | data formatting | bytes 1179648
  164.4 1.6 copy.10
  166.0 0.0 copy-done
  166.0 1.0 copy.11
Async XLA Ops:
  162.4 3.6 %copy-start = (bf16[96,6144]{1,0:T(8,128)(2,1)S(1)}, bf16[96,6144]{1,0:T(8,128)(2,1)}, u32[]{:S(2)}) copy-start(bf16[96,6144]{1,0:T(8,128)(2,1)} %get-tuple-element.8) | copy-start | bytes 3538948

commit v2 on v1

--- a/solution.py
+++ b/solution.py
@@ -12,20 +12,33 @@
 F32 = jnp.float32
 BF16 = jnp.bfloat16
 
-CHUNKS = 8
+WIDTH = 512
 
 root_coef = math.sqrt(2.0 / math.pi)
 
-RS1, RS2, RSY, AGY, AGX1, AGX2, Z1, Z2, Z3, Z4 = 0, 2, 4, 5, 6, 8, 10, 12, 14, 16
-COPIES = 18
+RS1, RS2, RSY, AG1, AG2, AG3, Z1, Z2, Z3, Z4 = 0, 2, 4, 5, 8, 12, 13, 15, 17, 19
+COPIES = 21
+
+PLAN = (
+    1, 2, 33, 384, 34, 65, 3, 97, 66, 35, 192, 129, 98, 4, 161, 67, 256, 130, 36, 193, 99, 5, 162, 288,
+    68, 224, 257, 131, 37, 194, 100, 320, 6, 163, 289, 69, 225, 258, 132, 38, 195, 352, 101, 321, 7,
+    164, 290, 70, 226, 259, 133, 39, 196, 353, 102, 322, 8, 165, 291, 71, 227, 260, 134, 40, 197, 354,
+    103, 323, 9, 166, 292, 72, 228, 261, 135, 41, 198, 355, 104, 324, 10, 167, 293, 73, 229, 262, 136,
+    42, 199, 356, 105, 325, 11, 168, 294, 74, 230, 263, 137, 43, 200, 357, 106, 326, 169, 295, 75, 231,
+    264, 138, 201, 358, 107, 327, 170, 296, 232, 265, 139, 202, 359, 328, 171, 297, 233, 266, 203, 360,
+    329, 298, 234, 267, 361, 330, 299, 235, 362, 331, 363,
+)
+STAGE_OF_INPUT_PART = 7
+LAST_INPUT_PART = [entry % 32 for entry in PLAN if entry // 32 == STAGE_OF_INPUT_PART][-1]
 
 
 def kernel(
     scale, chunks,
     tok_hbm, w_hbm, cot_hbm, act_hbm, ig_hbm, wg_hbm,
-    tok, tok_t, w, cot, part, r1, r2, y_out, y_in, own, hid, grad, z1_in, z_in,
+    tok, tok_t, w, cot, part, r1, r2, y_out, y_in, own, hid, grad, z1_in, z_in, direct_in,
     acc, ig_out, ig_in, ig_own, act, wg,
-    send, recv, col_send, col_recv, load_w, load_cot, load_tok, store_act, store_wg, store_ig,
+    send, recv, direct_send, direct_recv, col_send, col_recv, load_w, load_cot, load_tok,
+    store_act, store_wg, store_ig,
 ):
     width = w.shape[2]
     half = width // 2
@@ -38,6 +51,8 @@
     across = {"row": other_y * 4 + x}
     at = [lax.rem(dep + k, 8) for k in range(8)]
     up, down = {"dep": at[1]}, {"dep": at[7]}
+    row_peers = [(lax.rem(y + k // 4, 2), lax.rem(x + k % 4, 4)) for k in (6, 2, 5, 7, 1, 3, 4)]
+    row_from = [(lax.rem(y + k // 4, 2), lax.rem(x + 4 - k % 4, 4)) for k in (6, 2, 5, 7, 1, 3, 4)]
     col_peers = [{"col": lax.rem(col + j, 4)} for j in (1, 2, 3)]
 
     def columns(c):
@@ -57,13 +72,10 @@
     @pl.loop(0, chunks)
     def _(c):
         w_copy(c).start()
-
-    @pl.loop(0, chunks)
-    def _(c):
         cot_copy(c).start()
 
     barrier = pltpu.get_barrier_semaphore()
-    peers = [right, left, across, up, down] + col_peers
+    peers = [up, down] + [{"row": there_y * 4 + there_x} for there_y, there_x in row_peers] + col_peers
     for peer in peers:
         pl.semaphore_signal(barrier, inc=1, device_id=peer, device_id_type=MESH)
 
@@ -82,6 +94,22 @@
             device_id=device, device_id_type=MESH,
         )
 
+    def direct(k, source, target):
+        there_y, there_x = row_peers[k % 7]
+        return pltpu.make_async_remote_copy(
+            src_ref=source, dst_ref=target, send_sem=direct_send.at[k], recv_sem=direct_recv.at[k],
+            device_id={"row": there_y * 4 + there_x}, device_id_type=MESH,
+        )
+
+    def direct_scatter():
+        return [direct(k, part.at[0, *row_peers[k]], direct_in.at[k]) for k in range(7)]
+
+    def direct_gather():
+        return [direct(7 + k, hid.at[0, y, x], hid.at[0, y, x]) for k in range(7)]
+
+    def direct_gathered():
+        return [direct(7 + k, hid.at[0, *row_from[k]], hid.at[0, *row_from[k]]) for k in range(7)]
+
     def rs1(c):
         return (
             remote(c, RS1, part.at[c, :, xo, :, left_half], r1.at[c, 0], right),
@@ -97,20 +125,27 @@
     def rsy(c):
         return (remote(c, RSY, y_out.at[c], y_in.at[c], across),)
 
-    def agy(c):
-        return (remote(c, AGY, hid.at[c, y, x], hid.at[c, y, x], across),)
-
-    def agx1(c):
-        return (
-            remote(c, AGX1, hid.at[c, :, x], hid.at[c, :, x], right),
-            remote(c, AGX1 + 1, hid.at[c, :, x], hid.at[c, :, x], left),
-        )
-
-    def agx2(c):
-        return (
-            remote(c, AGX2, hid.at[c, :, xl, :, left_half], hid.at[c, :, xl, :, left_half], right),
-            remote(c, AGX2 + 1, hid.at[c, :, xr, :, right_half], hid.at[c, :, xr, :, right_half], left),
-        )
+    def block(c, which, there, device, columns=None):
+        ref = hid.at[c, *there] if columns is None else hid.at[c, *there, :, columns]
+        return remote(c, which, ref, ref, device)
+
+    def ag1(c, here=True):
+        return (
+            block(c, AG1, (y, x if here else xl), right),
+            block(c, AG1 + 1, (y, x if here else xr), left),
+            block(c, AG1 + 2, (y if here else other_y, x), across),
+        )
+
+    def ag2(c, here=True):
+        return (
+            block(c, AG2, (y, xl if here else xo), right, left_half),
+            block(c, AG2 + 1, (y, xr if here else xo), left, right_half),
+            block(c, AG2 + 2, (y if here else other_y, xl), across),
+            block(c, AG2 + 3, (y if here else other_y, xr), across),
+        )
+
+    def ag3(c, here=True):
+        return (block(c, AG3, (y if here else other_y, xo), across),)
 
     def z1(c):
         return (
@@ -151,10 +186,25 @@
     def f32(value):
         return value.astype(F32)
 
+    def product_of(c):
+        w_copy(c).wait()
+        value = jnp.dot(tok[...], w[c], preferred_element_type=F32).astype(BF16)
+        part[c] = value.reshape(part.shape[1:])
+
+    def finish(c, value):
+        square = value * value
+        tangent = jnp.tanh(root_coef * (value + 0.044715 * value * square))
+        slope = 0.5 * (1.0 + tangent) + 0.5 * value * (1.0 - tangent * tangent) * root_coef * (
+            1.0 + 3.0 * 0.044715 * square
+        )
+        cot_copy(c).wait()
+        hid[c, y, x] = (f32(cot[c]) * slope).astype(BF16)
+        start(direct_gather() if isinstance(c, int) else ag1(c))
+        act[c] = (0.5 * value * (1.0 + tangent)).astype(BF16)
+        act_copy(c).start()
+
     def project(c):
-        w_copy(c).wait()
-        block = jnp.dot(tok[...], w[c], preferred_element_type=F32).astype(BF16)
-        part[c] = block.reshape(part.shape[1:])
+        product_of(c)
         start(rs1(c))
 
     def row_second(c):
@@ -171,34 +221,25 @@
 
     def activate(c):
         arrived(rsy(c))
-        cot_copy(c).wait()
-        value = own[c] + f32(y_in[c])
-        square = value * value
-        tangent = jnp.tanh(root_coef * (value + 0.044715 * value * square))
-        slope = 0.5 * (1.0 + tangent) + 0.5 * value * (1.0 - tangent * tangent) * root_coef * (
-            1.0 + 3.0 * 0.044715 * square
-        )
-        hid[c, y, x] = (f32(cot[c]) * slope).astype(BF16)
-        start(agy(c))
-        act[c] = (0.5 * value * (1.0 + tangent)).astype(BF16)
-        act_copy(c).start()
-
-    def gather_first(c):
-        arrived((remote(c, AGY, hid.at[c, other_y, x], hid.at[c, other_y, x], across),))
-        start(agx1(c))
+        finish(c, own[c] + f32(y_in[c]))
 
     def gather_second(c):
-        arrived((
-            remote(c, AGX1, hid.at[c, :, xl], hid.at[c, :, xl], right),
-            remote(c, AGX1 + 1, hid.at[c, :, xr], hid.at[c, :, xr], left),
-        ))
-        start(agx2(c))
+        arrived(ag1(c, False)[:2])
+        start(ag2(c))
+
+    def gather_third(c):
+        arrived(ag2(c, False)[:2])
+        start(ag3(c))
 
     def weight_first(c):
-        arrived((
-            remote(c, AGX2, hid.at[c, :, xo, :, left_half], hid.at[c, :, xo, :, left_half], right),
-            remote(c, AGX2 + 1, hid.at[c, :, xo, :, right_half], hid.at[c, :, xo, :, right_half], left),
-        ))
+        @pl.when(c > 0)
+        def _():
+            arrived(ag1(c, False)[2:] + ag2(c, False)[2:] + ag3(c, False))
+
+        @pl.when(c == 0)
+        def _():
+            arrived(direct_gathered())
+
         rows = hid[c].reshape(-1, width)
         product = jnp.dot(tok_t[...], rows, preferred_element_type=F32)
         grad[c] = (product * scale).astype(BF16).reshape(grad.shape[1:])
@@ -208,7 +249,7 @@
         rows = hid[c].reshape(-1, width)
         acc[...] += lax.dot_general(rows, w[c], (((1,), (1,)), ((), ())), preferred_element_type=F32)
 
-        @pl.when(c == chunks - 1)
+        @pl.when(c == LAST_INPUT_PART)
         def _():
             ig_out[...] = acc[...].astype(BF16).reshape(ig_out.shape)
             for j in (1, 2, 3):
@@ -237,27 +278,68 @@
         wg[c] = (f32(grad[c, dep]) + f32(z_in[c, 2, 0]) + f32(z_in[c, 2, 1])).astype(BF16)
         wg_copy(c).start()
 
+        def sent(stages_of_chunk):
+            for copies in stages_of_chunk:
+                for copy in copies(c):
+                    copy.wait_send()
+
+        sent((z1, z2, z3, z4))
+
+        @pl.when(c > 0)
+        def _():
+            sent((rs1, rs2, rsy, ag1, ag2, ag3))
+
+        @pl.when(c == 0)
+        def _():
+            for copy in direct_scatter() + direct_gather():
+                copy.wait_send()
+
+        act_copy(c).wait()
+
+    def first_activate(_):
+        arrived(direct_scatter())
+        value = f32(part[0, y, x])
+        for k in range(7):
+            value = value + f32(direct_in[k])
+        finish(0, value)
+
     tok_copy().wait()
+    product_of(0)
+    pl.semaphore_wait(barrier, len(peers))
+    start(direct_scatter())
     tok_t[...] = tok[...].T
     acc[...] = jnp.zeros_like(acc)
-    pl.semaphore_wait(barrier, len(peers))
-
-    order = (
-        (weight_first, 2), (activate, 1), (project, 0), (input_part, 2),
-        (weight_third, 3), (gather_first, 1),
-        (weight_second, 2), (row_second, 0),
-        (weight_fourth, 3), (gather_second, 1), (row_across, 0), (weight_last, 4),
+
+    stages = (
+        project, row_second, row_across, activate, gather_second, gather_third, weight_first,
+        input_part, weight_second, weight_third, weight_fourth, weight_last, first_activate,
     )
-    slots = max(late for _, late in order)
-
-    @pl.loop(0, chunks + slots)
-    def _(t):
-        for stage, late in order:
-            c = t - late
-
-            @pl.when((c >= 0) & (c < chunks))
-            def _(stage=stage, c=c):
-                stage(c)
+
+    words = [
+        sum(entry * 512 ** k for k, entry in enumerate(PLAN[i:i + 3])) for i in range(0, len(PLAN), 3)
+    ]
+
+    @pl.loop(0, len(PLAN))
+    def _(i):
+        place, level = i // 3, words
+        while len(level) > 1:
+            odd = lax.rem(place, 2) == 1
+            pairs = [level[k:k + 2] for k in range(0, len(level), 2)]
+            level = [jnp.where(odd, pair[-1], pair[0]) for pair in pairs]
+            place = place // 2
+        within = lax.rem(i, 3)
+        word = jnp.where(within == 0, level[0], jnp.where(within == 1, level[0] // 512, level[0] // 262144))
+        entry = lax.rem(word, 512)
+        stage, c = entry // 32, lax.rem(entry, 32)
+
+        def dispatch(low, high):
+            if high - low == 1:
+                stages[low](c)
+                return
+            middle = (low + high) // 2
+            lax.cond(stage < middle, lambda: dispatch(low, middle), lambda: dispatch(middle, high))
+
+        dispatch(0, len(stages))
 
     for j in (1, 2, 3):
         col_copy(j).wait_recv()
@@ -268,10 +350,6 @@
 
     @pl.loop(0, chunks)
     def _(c):
-        for copies in (rs1, rs2, rsy, agy, agx1, agx2, z1, z2, z3, z4):
-            for copy in copies(c):
-                copy.wait_send()
-        act_copy(c).wait()
         wg_copy(c).wait()
 
     for j in (1, 2, 3):
@@ -279,18 +357,32 @@
     ig_copy().wait()
 
 
-def body(chunks, tokens_in, weight, cotangent):
+def publish(act_from, ig_from, wg_from, act_to, ig_to, wg_to, act, ig, wg, sem_in, sem_out):
+    inward, outward = [], []
+    for k, (source, held, target) in enumerate(((wg_from, wg, wg_to), (act_from, act, act_to), (ig_from, ig, ig_to))):
+        inward.append(pltpu.make_async_copy(source, held, sem_in.at[k]))
+        outward.append(pltpu.make_async_copy(held, target, sem_out.at[k]))
+    for copy in inward:
+        copy.start()
+    for copy, onward in zip(inward, outward):
+        copy.wait()
+        onward.start()
+    for copy in outward:
+        copy.wait()
+
+
+def body(tokens_in, weight, cotangent):
     tokens, features = tokens_in.shape[1:]
     hidden = weight.shape[1]
     own_tokens = cotangent.shape[1]
     scale = 1.0 / math.sqrt(tokens * lax.axis_size("dep"))
-    c, w = chunks, hidden // chunks
+    c, w = hidden // WIDTH, WIDTH
     h = w // 2
     own_features, col_tokens = features // 8, tokens // 4
     vmem = pltpu.VMEM
     dma = pltpu.SemaphoreType.DMA
-    return pl.pallas_call(
-        functools.partial(kernel, scale, chunks),
+    results = pl.pallas_call(
+        functools.partial(kernel, scale, c),
         out_shape=(
             jax.ShapeDtypeStruct((1, own_tokens, hidden), BF16),
             jax.ShapeDtypeStruct((1, col_tokens, features), BF16),
@@ -313,6 +405,7 @@
             vmem((c, 8, own_features, w), BF16),
             vmem((c, 2, own_features, h), BF16),
             vmem((c, 3, 2, own_features, w), BF16),
+            vmem((7, own_tokens, w), BF16),
             vmem((tokens, features), F32),
             vmem((4, col_tokens, features), BF16),
             vmem((3, col_tokens, features), BF16),
@@ -321,6 +414,8 @@
             vmem((c, own_features, w), BF16),
             dma((c, COPIES)),
             dma((c, COPIES)),
+            dma((14,)),
+            dma((14,)),
             dma((3,)),
             dma((3,)),
             dma((c,)),
@@ -339,11 +434,18 @@
             transcendentals=own_tokens * hidden,
         ),
     )(tokens_in, weight, cotangent)
+    return pl.pallas_call(
+        publish,
+        out_shape=tuple(jax.ShapeDtypeStruct(result.shape, result.dtype) for result in results),
+        in_specs=[pl.BlockSpec(memory_space=pl.ANY)] * 3,
+        out_specs=(pl.BlockSpec(memory_space=pl.ANY),) * 3,
+        scratch_shapes=[vmem(result.shape, result.dtype) for result in results] + [dma((3,)), dma((3,))],
+    )(*results)
 
 
 def solution(mesh):
     in_specs = (P("dep", None, "row"), P("row", "col"), P("dep", "row", "col"))
     out_specs = (P("dep", "row", "col"), P("dep", "col", "row"), P(("row", "dep"), "col"))
     return jax.shard_map(
-        functools.partial(body, CHUNKS), mesh=mesh, in_specs=in_specs, out_specs=out_specs, check_vma=False
+        body, mesh=mesh, in_specs=in_specs, out_specs=out_specs, check_vma=False
     )

time: 167 us -> 138 us (0.83)
  Pallas kernels: 162 us -> 137 us
  local copies, waits for them, and re-layouts: 4.61 us -> 0 us
    pallas_call x1 -> x2, Pallas kernels: 162 us -> 137 us  [the longest x1 134 us: body(): pl.pallas_call(functools.partial(kernel, scale, c), out_shape=(jax.ShapeD...]
    unnamed x5 -> x0, local copies, waits for them, and re-layouts: 4.61 us -> none
where the time goes in v2:
time: 138 us; the launch traced here: 137 us
  Pallas kernels  137 us (99%)
    pallas_call x1, Pallas kernels, body(): pl.pallas_call(functools.partial(kernel, scale, c), out_shape=(jax.ShapeD...  134 us

profile of v2, /device:TPU:32, one launch (start us, length us, event | category | flops | bytes accessed | tf_op | source)
XLA Modules:
  0.0 137.4 jit_solution(14946519363123875251)
XLA Ops:
  0.6 134.2 %shard_map.58 = (bf16[1,48,6144]{2,1,0:T(8,128)(2,1)}, bf16[1,96,768]{2,1,0:T(8,128)(2,1)}, bf16[96,6144]{1,0:T(8,128)(2,1)}) custom-call(bf16[1,384,768]{2,1,0:T(8,128)(2,1)} %tok_hbm.1, bf16[768,6144]{1,0:T(8,128)(2,1)} %w_hbm.1, bf16[1,48,6144]{2,1,0:T(8,128)(2,1)} %cot_hbm.1), custom_call_target="tpu_custom_call" | custom-call | flops 10871635968 | bytes 11206656 | tf_op jit(solution)/shard_map/pallas_call | solution.py:384
  134.9 2.6 %shard_map.59 = (bf16[1,48,6144]{2,1,0:T(8,128)(2,1)}, bf16[1,96,768]{2,1,0:T(8,128)(2,1)}, bf16[96,6144]{1,0:T(8,128)(2,1)}) custom-call(bf16[1,48,6144]{2,1,0:T(8,128)(2,1)} %get-tuple-element.6.act_from, bf16[1,96,768]{2,1,0:T(8,128)(2,1)} %get-tuple-element.7.ig_from, bf16[96,6144]{1,0:T(8,128)(2,1)} %get-tuple-element.8.wg_from), custom_call_target="tpu_custom_call" | custom-call | tf_op jit(solution)/shard_map/pallas_call | solution.py:437

commit v3 on v2

--- a/solution.py
+++ b/solution.py
@@ -25,8 +25,8 @@
     164, 290, 70, 226, 259, 133, 39, 196, 353, 102, 322, 8, 165, 291, 71, 227, 260, 134, 40, 197, 354,
     103, 323, 9, 166, 292, 72, 228, 261, 135, 41, 198, 355, 104, 324, 10, 167, 293, 73, 229, 262, 136,
     42, 199, 356, 105, 325, 11, 168, 294, 74, 230, 263, 137, 43, 200, 357, 106, 326, 169, 295, 75, 231,
-    264, 138, 201, 358, 107, 327, 170, 296, 232, 265, 139, 202, 359, 328, 171, 297, 233, 266, 203, 360,
-    329, 298, 234, 267, 361, 330, 299, 235, 362, 331, 363,
+    264, 138, 201, 358, 107, 327, 170, 296, 232, 265, 139, 202, 359, 328, 171, 297, 233, 266, 203, 235,
+    360, 329, 298, 234, 267, 361, 330, 299, 362, 331, 363,
 )
 STAGE_OF_INPUT_PART = 7
 LAST_INPUT_PART = [entry % 32 for entry in PLAN if entry // 32 == STAGE_OF_INPUT_PART][-1]
@@ -315,20 +315,22 @@
         input_part, weight_second, weight_third, weight_fourth, weight_last, first_activate,
     )
 
-    words = [
-        sum(entry * 512 ** k for k, entry in enumerate(PLAN[i:i + 3])) for i in range(0, len(PLAN), 3)
-    ]
-
-    @pl.loop(0, len(PLAN))
-    def _(i):
-        place, level = i // 3, words
-        while len(level) > 1:
+    idle = 32 * len(stages)
+    padded = list(PLAN) + [idle] * (-len(PLAN) % 12)
+    words = [sum(entry * 512 ** k for k, entry in enumerate(padded[i:i + 3])) for i in range(0, len(padded), 3)]
+    stages = stages + (lambda c: None,)
+
+    def pick(place, values):
+        while len(values) > 1:
             odd = lax.rem(place, 2) == 1
-            pairs = [level[k:k + 2] for k in range(0, len(level), 2)]
-            level = [jnp.where(odd, pair[-1], pair[0]) for pair in pairs]
+            pairs = [values[k:k + 2] for k in range(0, len(values), 2)]
+            values = [jnp.where(odd, pair[-1], pair[0]) for pair in pairs]
             place = place // 2
-        within = lax.rem(i, 3)
-        word = jnp.where(within == 0, level[0], jnp.where(within == 1, level[0] // 512, level[0] // 262144))
+        return values[0]
+
+    def perform(i, group_words):
+        word, within = pick(i // 3, group_words), lax.rem(i, 3)
+        word = jnp.where(within == 0, word, jnp.where(within == 1, word // 512, word // 262144))
         entry = lax.rem(word, 512)
         stage, c = entry // 32, lax.rem(entry, 32)
 
@@ -340,6 +342,11 @@
             lax.cond(stage < middle, lambda: dispatch(low, middle), lambda: dispatch(middle, high))
 
         dispatch(0, len(stages))
+
+    @pl.loop(0, len(padded) // 12)
+    def _(group):
+        group_words = [pick(group, words[k::4]) for k in range(4)]
+        pl.loop(0, 12)(lambda i: perform(i, group_words))
 
     for j in (1, 2, 3):
         col_copy(j).wait_recv()

time: 138 us -> 138 us (level)
  no operation moved by 1% of the time
where the time goes in v3:
time: 138 us; the launch traced here: 137 us
  Pallas kernels  137 us (99%)
    pallas_call x1, Pallas kernels, body(): pl.pallas_call(functools.partial(kernel, scale, c), out_shape=(jax.ShapeD...  134 us

profile of v3, /device:TPU:32, one launch (start us, length us, event | category | flops | bytes accessed | tf_op | source)
XLA Modules:
  0.0 137.4 jit_solution(5017128319608259257)
XLA Ops:
  0.6 134.2 %shard_map.58 = (bf16[1,48,6144]{2,1,0:T(8,128)(2,1)}, bf16[1,96,768]{2,1,0:T(8,128)(2,1)}, bf16[96,6144]{1,0:T(8,128)(2,1)}) custom-call(bf16[1,384,768]{2,1,0:T(8,128)(2,1)} %tok_hbm.1, bf16[768,6144]{1,0:T(8,128)(2,1)} %w_hbm.1, bf16[1,48,6144]{2,1,0:T(8,128)(2,1)} %cot_hbm.1), custom_call_target="tpu_custom_call" | custom-call | flops 10871635968 | bytes 11206656 | tf_op jit(solution)/shard_map/pallas_call | solution.py:391
  134.8 2.6 %shard_map.59 = (bf16[1,48,6144]{2,1,0:T(8,128)(2,1)}, bf16[1,96,768]{2,1,0:T(8,128)(2,1)}, bf16[96,6144]{1,0:T(8,128)(2,1)}) custom-call(bf16[1,48,6144]{2,1,0:T(8,128)(2,1)} %get-tuple-element.6.act_from, bf16[1,96,768]{2,1,0:T(8,128)(2,1)} %get-tuple-element.7.ig_from, bf16[96,6144]{1,0:T(8,128)(2,1)} %get-tuple-element.8.wg_from), custom_call_target="tpu_custom_call" | custom-call | tf_op jit(solution)/shard_map/pallas_call | solution.py:444

commit v4 on v2

--- a/solution.py
+++ b/solution.py
@@ -25,8 +25,8 @@
     164, 290, 70, 226, 259, 133, 39, 196, 353, 102, 322, 8, 165, 291, 71, 227, 260, 134, 40, 197, 354,
     103, 323, 9, 166, 292, 72, 228, 261, 135, 41, 198, 355, 104, 324, 10, 167, 293, 73, 229, 262, 136,
     42, 199, 356, 105, 325, 11, 168, 294, 74, 230, 263, 137, 43, 200, 357, 106, 326, 169, 295, 75, 231,
-    264, 138, 201, 358, 107, 327, 170, 296, 232, 265, 139, 202, 359, 328, 171, 297, 233, 266, 203, 360,
-    329, 298, 234, 267, 361, 330, 299, 235, 362, 331, 363,
+    264, 138, 201, 358, 107, 327, 170, 296, 232, 265, 139, 202, 359, 328, 171, 297, 233, 266, 203, 235,
+    360, 329, 298, 234, 267, 361, 330, 299, 362, 331, 363,
 )
 STAGE_OF_INPUT_PART = 7
 LAST_INPUT_PART = [entry % 32 for entry in PLAN if entry // 32 == STAGE_OF_INPUT_PART][-1]
@@ -90,7 +90,8 @@
 
     def remote(c, which, source, target, device):
         return pltpu.make_async_remote_copy(
-            src_ref=source, dst_ref=target, send_sem=send.at[c, which], recv_sem=recv.at[c, which],
+            src_ref=source, dst_ref=target, send_sem=send.at[which],
+            recv_sem=recv.at[c if isinstance(c, jax.Array) else 0, which],
             device_id=device, device_id_type=MESH,
         )
 
@@ -277,24 +278,6 @@
         arrived(z4(c))
         wg[c] = (f32(grad[c, dep]) + f32(z_in[c, 2, 0]) + f32(z_in[c, 2, 1])).astype(BF16)
         wg_copy(c).start()
-
-        def sent(stages_of_chunk):
-            for copies in stages_of_chunk:
-                for copy in copies(c):
-                    copy.wait_send()
-
-        sent((z1, z2, z3, z4))
-
-        @pl.when(c > 0)
-        def _():
-            sent((rs1, rs2, rsy, ag1, ag2, ag3))
-
-        @pl.when(c == 0)
-        def _():
-            for copy in direct_scatter() + direct_gather():
-                copy.wait_send()
-
-        act_copy(c).wait()
 
     def first_activate(_):
         arrived(direct_scatter())
@@ -348,8 +331,19 @@
     ig_own[...] = (mine + f32(ig_in[0]) + f32(ig_in[1]) + f32(ig_in[2])).astype(BF16)
     ig_copy().start()
 
+    rest, every = pl.ds(1, chunks - 1), pl.ds(0, chunks)
+    for copies in (rs1, rs2, rsy, ag1, ag2, ag3):
+        for copy in copies(rest):
+            copy.wait_send()
+    for copies in (z1, z2, z3, z4):
+        for copy in copies(every):
+            copy.wait_send()
+    for copy in direct_scatter() + direct_gather():
+        copy.wait_send()
+
     @pl.loop(0, chunks)
     def _(c):
+        act_copy(c).wait()
         wg_copy(c).wait()
 
     for j in (1, 2, 3):
@@ -412,7 +406,7 @@
             vmem((col_tokens, features), BF16),
             vmem((c, own_tokens, w), BF16),
             vmem((c, own_features, w), BF16),
-            dma((c, COPIES)),
+            dma((COPIES,)),
             dma((c, COPIES)),
             dma((14,)),
             dma((14,)),

time: 138 us -> 136 us (0.986)
  Pallas kernels: 137 us -> 135 us
    pallas_call x1, Pallas kernels: 134 us -> 132 us  [body(): pl.pallas_call(functools.partial(kernel, scale, c), out_shape=(jax.ShapeD...]
where the time goes in v4:
time: 136 us; the launch traced here: 135 us
  Pallas kernels  135 us (99%)
    pallas_call x1, Pallas kernels, body(): pl.pallas_call(functools.partial(kernel, scale, c), out_shape=(jax.ShapeD...  132 us

profile of v4, /device:TPU:32, one launch (start us, length us, event | category | flops | bytes accessed | tf_op | source)
XLA Modules:
  0.0 135.2 jit_solution(6027726821614197611)
XLA Ops:
  0.6 132.0 %shard_map.58 = (bf16[1,48,6144]{2,1,0:T(8,128)(2,1)}, bf16[1,96,768]{2,1,0:T(8,128)(2,1)}, bf16[96,6144]{1,0:T(8,128)(2,1)}) custom-call(bf16[1,384,768]{2,1,0:T(8,128)(2,1)} %tok_hbm.1, bf16[768,6144]{1,0:T(8,128)(2,1)} %w_hbm.1, bf16[1,48,6144]{2,1,0:T(8,128)(2,1)} %cot_hbm.1), custom_call_target="tpu_custom_call" | custom-call | flops 10871635968 | bytes 11206656 | tf_op jit(solution)/shard_map/pallas_call | solution.py:378
  132.6 2.6 %shard_map.59 = (bf16[1,48,6144]{2,1,0:T(8,128)(2,1)}, bf16[1,96,768]{2,1,0:T(8,128)(2,1)}, bf16[96,6144]{1,0:T(8,128)(2,1)}) custom-call(bf16[1,48,6144]{2,1,0:T(8,128)(2,1)} %get-tuple-element.6.act_from, bf16[1,96,768]{2,1,0:T(8,128)(2,1)} %get-tuple-element.7.ig_from, bf16[96,6144]{1,0:T(8,128)(2,1)} %get-tuple-element.8.wg_from), custom_call_target="tpu_custom_call" | custom-call | tf_op jit(solution)/shard_map/pallas_call | solution.py:431
